TPU v7x, 32 devices: a whole 2x2x4 slice. The times are simulated.
32 devices in a mesh: maps: 2 (over y), row: 4 (over z), col: 4 (over x, core).
Axes of the slice: x: 2, y: 2, z: 4, core: 2. Of those that a mesh axis runs over, the one named last changes fastest.
Arguments:
- tokens: bfloat16 [64, 512, 576], P(('maps', 'row'), 'col'), parts along dimension 0, may hold values from -6 to 6
- w_qkv: bfloat16 [576, 1728], replicated, may hold values from -0.25 to 0.25
- pool_kernel: bfloat16 [2, 9, 9, 72], replicated, may hold values from -0.625 to 0.625
- key_gain: float32 [72], replicated, may hold values from 1.5 to 80
- value_gain: float32 [72], replicated, may hold values from 0.5 to 2
- w_proj: bfloat16 [576, 576], replicated, may hold values from -0.25 to 0.25
- w_up: bfloat16 [576, 2304], replicated, may hold values from -0.25 to 0.25
- w_down: bfloat16 [2304, 576], replicated, may hold values from -0.125 to 0.125
Outputs:
- block_out: bfloat16 [64, 512, 576], P(('maps', 'row'), 'col'), parts along dimension 0
There are 2 independent parts, one for each index of `maps`. A program takes and returns all parts, laid end to end along the dimension named above; an argument that names none is the same for every part. Nothing has to cross between parts.
All inputs are finite; a program needn't handle non-finite values.
Results may differ from a plain program's by a relative error of at most 0.0095.
The roundings to bfloat16 on the way count: a program that leaves them out, or rounds other values in their place, can miss the bound.
Values may be sent and summed in bfloat16 or wider, within the bound.
A program may use at most 128 MiB of HBM per device.

v0:
```python
import math

import jax
import jax.numpy as jnp
from jax import lax
from jax.sharding import PartitionSpec as P

HEADS = 8
STRIDE = 8


EPS = 1e-06


def from_behind(block, axis, distance):
    devices = range(lax.axis_size(axis))
    route = [(i - distance, i) for i in devices if i - distance in devices]
    return lax.ppermute(block, axis, route)


def layer_norm(values):
    mean = jnp.mean(values, axis=-1, keepdims=True)
    centred = values - mean
    spread = jnp.mean(centred * centred, axis=-1, keepdims=True)
    return centred * lax.rsqrt(spread + EPS)


def pool(framed, kernel, heads, stride, pads):
    head_dim = kernel.shape[-1]
    span = kernel.shape[1]
    channels = 2 * head_dim * heads
    full = jnp.concatenate(
        [jnp.tile(kernel[0], (1, 1, heads)), jnp.tile(kernel[1], (1, 1, heads))], axis=-1
    )
    full = full.reshape(span, span, 1, channels)
    result = lax.conv_general_dilated(
        framed[None],
        full,
        (stride, stride),
        pads,
        dimension_numbers=("NHWC", "HWIO", "NHWC"),
        feature_group_count=channels,
        preferred_element_type=jnp.float32,
    )
    return result[0]


def norm_pooled(pooled, key_gain, value_gain, heads):
    count = pooled.shape[0]
    head_dim = key_gain.shape[0]
    split = pooled.reshape(count, 2, heads, head_dim)
    gains = jnp.stack([key_gain, value_gain]).reshape(1, 2, 1, head_dim)
    return (layer_norm(split) * gains).reshape(count, 2 * heads * head_dim).astype(jnp.bfloat16)


def finish_block(query_block, token_block, keys, values, w_proj, w_up, w_down, heads):
    count, width = query_block.shape
    head_dim = width // heads
    query = query_block.reshape(count, heads, head_dim)
    scores = jnp.einsum(
        "qhd,khd->hqk", query, keys, preferred_element_type=jnp.float32
    ) * head_dim ** (-0.5)
    top = jnp.max(scores, axis=-1, keepdims=True)
    weights = jnp.exp(scores - top)
    total = jnp.sum(weights, axis=-1)
    probs = weights.astype(jnp.bfloat16)
    mixed = jnp.einsum("hqk,khd->qhd", probs, values, preferred_element_type=jnp.float32)
    mixed = mixed / jnp.transpose(total)[:, :, None] + query.astype(jnp.float32)
    attended = mixed.reshape(count, width).astype(jnp.bfloat16)
    residual = (
        token_block.astype(jnp.float32)
        + jnp.dot(attended, w_proj, preferred_element_type=jnp.float32)
    ).astype(jnp.bfloat16)
    renormed = layer_norm(residual.astype(jnp.float32)).astype(jnp.bfloat16)
    hidden_act = jax.nn.gelu(
        jnp.dot(renormed, w_up, preferred_element_type=jnp.float32), approximate=False
    ).astype(jnp.bfloat16)
    return (
        residual.astype(jnp.float32)
        + jnp.dot(hidden_act, w_down, preferred_element_type=jnp.float32)
    ).astype(jnp.bfloat16)


def per_device(tokens, w_qkv, pool_kernel, key_gain, value_gain, w_proj, w_up, w_down):
    rows, cols, width = tokens.shape
    heads = HEADS
    head_dim = width // heads
    reach = pool_kernel.shape[1] // 2
    count = rows * cols
    flat = tokens.reshape(count, width)
    normed = layer_norm(flat.astype(jnp.float32)).astype(jnp.bfloat16)
    qkv = jnp.dot(normed, w_qkv, preferred_element_type=jnp.float32).astype(jnp.bfloat16)
    query = qkv[:, :width]
    keyval = qkv[:, width:].reshape(rows, cols, 2 * width)
    no_pad = ((0, 0), (0, 0))
    side = from_behind(keyval[:, cols - reach :], "col", 1)
    widened = jnp.concatenate([side, keyval], axis=1)
    upper = from_behind(widened[rows - reach :], "row", 1)
    framed = jnp.concatenate([upper, widened], axis=0)
    pooled = pool(framed, pool_kernel, heads, STRIDE, no_pad)
    pooled = pooled.reshape(-1, 2 * width)
    pooled_kv = norm_pooled(pooled, key_gain, value_gain, heads)
    gathered = lax.all_gather(pooled_kv, ("row", "col"), axis=0, tiled=True)
    keys = gathered[:, :width].reshape(-1, heads, head_dim)
    values = gathered[:, width:].reshape(-1, heads, head_dim)
    block = math.gcd(count, 512)

    def finish(pair):
        return finish_block(pair[0], pair[1], keys, values, w_proj, w_up, w_down, heads)

    result = lax.map(
        finish,
        (query.reshape(count // block, block, width), flat.reshape(count // block, block, width)),
    )
    return result.reshape(rows, cols, width)


def solution(mesh):
    in_specs = (P(("maps", "row"), "col", None), P(), P(), P(), P(), P(), P(), P())
    out_specs = P(("maps", "row"), "col", None)
    return jax.shard_map(
        per_device, mesh=mesh, in_specs=in_specs, out_specs=out_specs, check_vma=False
    )
```

profile of v0, /device:TPU:0, one launch (start us, length us, event | category | flops | bytes accessed | tf_op | source)
XLA Modules:
  0.0 264.9 jit_solution(8128160907097918708)
XLA Ops:
  0.0 1.6 convert_reduce_fusion.1
  1.6 1.6 fusion.90
  3.2 4.6 %convolution_convert_fusion = bf16[1024,1728]{0,1:T(8,128)(2,1)S(1)} fusion(bf16[576,1728]{1,0:T(8,128)(2,1)S(1)} %copy-done, f32[1024]{0:T(1024)S(1)} %rsqrt_bitcast_fusion, f32[1024]{0:T(1024)S(1)} %get-tuple-element.117, bf16[8,128,576]{1,2,0:T(8,128)(2,1)} %param.10), kind=kOutput, calls=%fused_computation.86 | convolution fusion | flops 2042560512 | bytes 6717440 | tf_op jit(solution)/shard_map/dot_general | solution.py:92
  7.8 1.7 copy-done.3
  9.6 1.6 slice.35
  11.2 4.3 %copy.65 = bf16[1024,1152]{1,0:T(8,128)(2,1)} copy(bf16[1024,1152]{0,1:T(8,128)(2,1)} %slice.35) | data formatting | bytes 4718592 | tf_op jit(solution)/shard_map/reshape | solution.py:94
  15.5 1.0 slice.36
  16.5 2.5 collective-permute-start
  19.9 1.6 pad_maximum_fusion
  21.5 1.5 copy.50
  23.0 5.4 %collective-permute-start.1 = (bf16[4,132,1152]{2,0,1:T(4,128)(2,1)}, bf16[4,132,1152]{2,0,1:T(4,128)(2,1)}, u32[]{:S(2)}, u32[]{:S(2)}) collective-permute-start(bf16[4,132,1152]{2,0,1:T(4,128)(2,1)} %copy.50), channel_id=1, source_target_pairs={{0,4},{4,8},{8,12},{1,5},{5,9},{9,13},{2,6},{6,10},{10,14},{3,7},{... | collective-permute-start | bytes 3649544 | tf_op jit(solution)/shard_map/ppermute | solution.py:18
  28.4 1.9 copy.46
  31.0 1.1 tile.22
  32.9 1.8 tile.25
  34.8 1.1 copy.79
  35.9 2.8 %reshape_reshape.3 = bf16[2,512,576]{1,0,2:T(2,128)(2,1)S(1)} reshape(bf16[8,128,576]{1,0,2:T(8,128)(2,1)} %copy.46) | data formatting | bytes 2359296 | tf_op jit(solution)/shard_map/reshape;reshape | solution.py:113
  38.6 1.2 copy.60
  39.9 1.2 maximum_bitcast_fusion.1
  41.1 12.3 %collective-permute-done.1 = bf16[4,132,1152]{2,0,1:T(4,128)(2,1)} collective-permute-done((bf16[4,132,1152]{2,0,1:T(4,128)(2,1)}, bf16[4,132,1152]{2,0,1:T(4,128)(2,1)}, u32[]{:S(2)}, u32[]{:S(2)}) %collective-permute-start.1) | collective-permute-done | bytes 1216544 | tf_op jit(solution)/shard_map/ppermute | solution.py:18
  53.4 1.4 copy.51
  54.9 1.6 maximum_bitcast_fusion
  57.2 0.9 copy.53
  58.6 131.1 %fusion.93 = f32[1,8,3,1152]{3,1,2,0:T(8,128)S(1)} fusion(bf16[12,1,7,8,1152]{4,2,3,0,1:T(8,128)(2,1)S(1)} %slice.37, bf16[12,1,8,24,1152]{4,2,3,0,1:T(8,128)(2,1)S(1)} %copy.53, bf16[9,9,1,1152]{3,1,0,2:T(8,128)(2,1)S(1)} %maximum_bitcast_fusion.1, pred[8,3]{0,1:T(4,128)(4,1)S(1)} %copy-done.9), kind=kOutput, calls=%fused_computation.97 | convolution fusion | flops 25740288 | bytes 7153944 | tf_op jit(solution)/shard_map/conv_general_dilated | solution.py:36
  191.0 25.1 %all_gather.3 = bf16[256,1152]{1,0:T(8,128)(2,1)S(1)} all-gather(bf16[16,1152]{1,0:T(8,128)(2,1)S(1)} %fusion.102), channel_id=1, replica_groups=mesh['maps'=2,'row'=4,'col'=4] {'row','col'}, dimensions={0}, use_global_device_ids=true | all-gather | bytes 626688 | tf_op jit(solution)/shard_map/all_gather | solution.py:103
  216.6 41.7 %while.10 = (s32[]{:T(128)}, bf16[2,512,576]{1,2,0:T(8,128)(2,1)}, bf16[2,512,576]{1,2,0:T(8,128)(2,1)}, bf16[2,512,576]{1,2,0:T(8,128)(2,1)}, bf16[256,8,72]{0,...) while((s32[]{:T(128)}, bf16[2,512,576]{1,2,0:T(8,128)(2,1)}, ...), condition=%wide.region_9.10_spmd, body=%wide.region_4.9_spmd.sunk | while | flops 3450593792 | bytes 33696420 | solution.py:111
  216.8 1.1 constant_dynamic-slice_fusion.2
  221.8 15.8 %fusion.143 = bf16[2,512,576]{1,2,0:T(8,128)(2,1)} fusion(bf16[2,512,576]{1,2,0:T(8,128)(2,1)} %get-tuple-element.195, s32[]{:T(128)} %get-tuple-element.194, bf16[2304,576]{0,1:T(8,128)(2,1)} %get-tuple-element.212, bf16[512,576]{0,1:T(8,128)(2,1)S(1)} %get-tuple-element.182, bf16[576,2304]{1,0:T(8,128)(2,1)} %get-tuple-element.211, ...), kind=kOutput, calls=%fused_computation.37.clone.1 | convolution fusion | flops 2796650496 | bytes 7082496 | tf_op jit(solution)/shard_map/while/body/eval_jaxpr/dot_general | solution.py:80
  237.6 1.1 constant_dynamic-slice_fusion.2
  242.6 15.8 %fusion.143 = bf16[2,512,576]{1,2,0:T(8,128)(2,1)} fusion(bf16[2,512,576]{1,2,0:T(8,128)(2,1)} %get-tuple-element.195, s32[]{:T(128)} %get-tuple-element.194, bf16[2304,576]{0,1:T(8,128)(2,1)} %get-tuple-element.212, bf16[512,576]{0,1:T(8,128)(2,1)S(1)} %get-tuple-element.182, bf16[576,2304]{1,0:T(8,128)(2,1)} %get-tuple-element.211, ...), kind=kOutput, calls=%fused_computation.37.clone.1 | convolution fusion | flops 2796650496 | bytes 7082496 | tf_op jit(solution)/shard_map/while/body/eval_jaxpr/dot_general | solution.py:80
  258.4 2.5 copy.62
  260.9 1.6 reshape.111
  262.5 2.4 copy.63
  (67 shorter events, 13.0 us)
Async XLA Ops:
  0.0 3.2 %copy-start = (bf16[576,1728]{1,0:T(8,128)(2,1)S(1)}, bf16[576,1728]{1,0:T(8,128)(2,1)}, u32[]{:S(2)}) copy-start(bf16[576,1728]{1,0:T(8,128)(2,1)} %param.11) | copy-start | bytes 5971972
  7.8 1.8 copy-start.3
  16.5 11.9 %copy-start.2 = (bf16[8,128,576]{1,2,0:T(8,128)(2,1)S(1)}, bf16[8,128,576]{1,2,0:T(8,128)(2,1)}, u32[]{:S(2)}) copy-start(bf16[8,128,576]{1,2,0:T(8,128)(2,1)} %param.10) | copy-start | bytes 3538948
  16.5 3.4 %collective-permute-start = (bf16[8,4,1152]{2,1,0:T(4,128)(2,1)S(1)}, bf16[8,4,1152]{2,1,0:T(4,128)(2,1)S(1)}, u32[]{:S(2)}, u32[]{:S(2)}) collective-permute-start(bf16[8,4,1152]{2,1,0:T(4,128)(2,1)S(1)} %slice.36), channel_id=1, source_target_pairs={{0,1},{1,2},{2,3},{4,5},{5,6},{6,7},{8,9},{9,10},{10,11},{12,13},{... | collective-permute-start | bytes 221192 | tf_op jit(solution)/shard_map/ppermute | solution.py:18
  21.5 8.8 %copy-start.5 = (bf16[2,9,9,72]{3,0,2,1:T(2,128)(2,1)S(1)}, bf16[2,9,9,72]{3,0,2,1:T(2,128)(2,1)}, u32[]{:S(2)}) copy-start(bf16[2,9,9,72]{3,0,2,1:T(2,128)(2,1)} %param.12) | copy-start | bytes 69988
  21.5 13.2 %copy-start.6 = (f32[72]{0:T(128)S(1)}, f32[72]{0:T(128)}, u32[]{:S(2)}) copy-start(f32[72]{0:T(128)} %param.14) | copy-start | bytes 868
  21.5 13.2 %copy-start.7 = (f32[72]{0:T(128)S(1)}, f32[72]{0:T(128)}, u32[]{:S(2)}) copy-start(f32[72]{0:T(128)} %param.13) | copy-start | bytes 868
  21.5 13.3 %slice-start = ((bf16[1024,1728]{0,1:T(8,128)(2,1)}), bf16[1024,576]{0,1:T(8,128)(2,1)S(1)}, s32[]{:S(2)}) async-start(bf16[1024,1728]{0,1:T(8,128)(2,1)} %copy-done.3), calls=%async_computation | async-start | bytes 2359296 | tf_op jit(solution)/shard_map/slice | solution.py:93
  23.0 30.4 %collective-permute-start.1 = (bf16[4,132,1152]{2,0,1:T(4,128)(2,1)}, bf16[4,132,1152]{2,0,1:T(4,128)(2,1)}, u32[]{:S(2)}, u32[]{:S(2)}) collective-permute-start(bf16[4,132,1152]{2,0,1:T(4,128)(2,1)} %copy.50), channel_id=1, source_target_pairs={{0,4},{4,8},{8,12},{1,5},{5,9},{9,13},{2,6},{6,10},{10,14},{3,7},{... | collective-permute-start | bytes 3649544 | tf_op jit(solution)/shard_map/ppermute | solution.py:18
  39.9 15.0 %copy-start.1 = (bf16[1024,1152]{1,0:T(8,128)(2,1)S(1)}, bf16[1024,1152]{1,0:T(8,128)(2,1)}, u32[]{:S(2)}) copy-start(bf16[1024,1152]{1,0:T(8,128)(2,1)} %copy.65) | copy-start | bytes 7077892
  57.2 1.4 copy-start.9
  219.4 1.3 copy-start.4
  219.5 1.5 copy-start.8
  240.2 1.3 copy-start.4
  240.2 1.5 copy-start.8
where the time goes:
time: 266 us; the launch traced here: 265 us
  matrix products  172 us (65%)
  local copies, waits for them, and re-layouts  36.4 us (14%)
  blocking collectives  25.1 us (9%)
  waiting for transfers between devices  13.2 us (5%)
  other arithmetic  9.83 us (4%)
  starting transfers between devices  7.86 us (3%)
    conv_general_dilated x1, matrix products, pool(): lax.conv_general_dilated(framed[None], full, (stride, stride), pads, dime...  131 us
    dot_general x2, matrix products, finish_block(): jnp.dot(hidden_act, w_down, preferred_element_type=jnp.float32)  31.6 us
    all_gather x1, blocking collectives, per_device(): gathered = lax.all_gather(pooled_kv, ('row', 'col'), axis=0, tiled=True)  25.1 us
    ppermute x2, waiting for transfers between devices, from_behind(): return lax.ppermute(block, axis, route)  13.2 us
    ppermute x2, starting transfers between devices, from_behind(): return lax.ppermute(block, axis, route)  7.86 us
  transfers between devices with their start and end apart: 2, of which 2 were waited for; matrix products, arithmetic and copies ran while one was open for 5% of the time, Pallas kernels for 0%

commit v1 on v0

v1 whole, which is shorter than its diff:
```python
import functools
import math

import jax
import jax.numpy as jnp
from jax import lax
from jax.experimental import pallas as pl
from jax.experimental.pallas import tpu as pltpu
from jax.sharding import PartitionSpec as P

HEADS = 8
STRIDE = 8
EPS = 1e-06
LANES = 128
MESH = pl.DeviceIdType.MESH
F32 = jnp.float32
BF16 = jnp.bfloat16


def layer_norm(values):
    mean = jnp.mean(values, axis=-1, keepdims=True)
    centred = values - mean
    spread = jnp.mean(centred * centred, axis=-1, keepdims=True)
    return centred * lax.rsqrt(spread + EPS)


def spread_matrix(head_dim, width, heads, shift, dtype):
    feature = lax.broadcasted_iota(jnp.int32, (head_dim, width), 0)
    lane = lax.broadcasted_iota(jnp.int32, (head_dim, width), 1) - shift
    hit = lane == feature
    for head in range(1, heads):
        hit = hit | (lane == feature + head * head_dim)
    return jnp.where(hit, 1.0, 0.0).astype(dtype)


def pooled_keys_kernel(
    rows_n, cols_n, heads,
    tokens_ref, w_ref, pool_ref, key_gain_ref, value_gain_ref,
    q_ref, gathered_ref,
    normed, keyval, taps, own, blocks,
    down_out, down_in, diag_out, diag_in, right_out, right_in,
    halo_send, halo_recv, send_sem, recv_sem,
):
    count, width = tokens_ref.shape
    head_dim = width // heads
    cols = count // STRIDE
    groups = cols // STRIDE
    span = pool_ref.shape[1]
    reach = span // 2
    aligned = width // LANES * LANES
    shift = width - aligned
    wide = shift + 2 * width
    row, col = lax.axis_index("row"), lax.axis_index("col")
    has_up, has_down = row > 0, row < rows_n - 1
    has_left, has_right = col > 0, col < cols_n - 1
    to_diag = jnp.logical_and(has_down, has_right)
    from_diag = jnp.logical_and(has_up, has_left)

    barrier = pltpu.get_barrier_semaphore()
    for step in range(1, rows_n):
        pl.semaphore_signal(
            barrier, inc=1, device_id={"row": lax.rem(row + step, rows_n)}, device_id_type=MESH)
    for step in range(1, cols_n):
        pl.semaphore_signal(
            barrier, inc=1, device_id={"col": lax.rem(col + step, cols_n)}, device_id_type=MESH)

    @pl.when(to_diag)
    def _():
        pl.semaphore_signal(
            barrier, inc=1, device_id={"row": row + 1, "col": col + 1}, device_id_type=MESH)

    @pl.when(from_diag)
    def _():
        pl.semaphore_signal(
            barrier, inc=1, device_id={"row": row - 1, "col": col - 1}, device_id_type=MESH)

    key_spread = spread_matrix(head_dim, shift + width, heads, shift, BF16)
    value_spread = spread_matrix(head_dim, width, heads, 0, BF16)
    for a in range(span):
        line = jnp.concatenate(
            [
                jnp.dot(pool_ref[0, a], key_spread, preferred_element_type=F32),
                jnp.dot(pool_ref[1, a], value_spread, preferred_element_type=F32),
            ],
            axis=-1,
        )
        below = jnp.zeros((STRIDE - reach - 1, wide), F32)
        above = jnp.zeros((STRIDE - reach, wide), F32)
        taps[0, a] = jnp.concatenate([line[reach:], below], axis=0)
        taps[1, a] = jnp.concatenate([above, line[:reach]], axis=0)

    def project(first, last):
        for at in range(first, last):
            line = pl.ds(at * cols, cols)
            normed[line, :] = layer_norm(tokens_ref[line, :].astype(F32)).astype(BF16)
        part = pl.ds(first * cols, (last - first) * cols)
        keyval[part, :] = jnp.dot(
            normed[part, :], w_ref[:, aligned:], preferred_element_type=F32).astype(BF16)

    def pool(first, last, offset, here, beyond):
        for start in range(0, wide, LANES):
            lanes = slice(start, min(start + LANES, wide))
            low, high = None, None
            for at in range(first, last):
                values = keyval[at * cols:(at + 1) * cols, lanes].astype(F32)
                values = values.reshape(groups, STRIDE, values.shape[-1])
                one = values * taps[0, at + offset, :, lanes][None]
                two = values * taps[1, at + offset, :, lanes][None]
                low = one if low is None else low + one
                high = two if high is None else high + two
            moved = jnp.concatenate([jnp.zeros_like(high[:1]), high[:-1]], axis=0)
            here[:, lanes] = jnp.sum(low + moved, axis=1)
            beyond[:, lanes] = jnp.sum(high[-1], axis=0, keepdims=True)

    def halo(at, source, target, device):
        return pltpu.make_async_remote_copy(
            src_ref=source, dst_ref=target, send_sem=halo_send.at[at], recv_sem=halo_recv.at[at],
            device_id=device, device_id_type=MESH)

    down = halo(0, down_out, down_in, {"row": lax.rem(row + 1, rows_n)})
    diag = halo(1, diag_out, diag_in,
                {"row": lax.rem(row + 1, rows_n), "col": lax.rem(col + 1, cols_n)})
    right = halo(2, right_out, right_in, {"col": lax.rem(col + 1, cols_n)})

    project(reach, STRIDE)
    pool(reach, STRIDE, -reach, down_out, diag_out)
    pl.semaphore_wait(
        barrier, rows_n - 1 + cols_n - 1 + to_diag.astype(jnp.int32) + from_diag.astype(jnp.int32))
    pl.when(has_down)(down.start)
    pl.when(to_diag)(diag.start)
    project(0, reach)
    pool(0, reach + 1, reach, own, right_out)
    pl.when(has_right)(right.start)

    q_ref[:, :aligned] = jnp.dot(
        normed[...], w_ref[:, :aligned], preferred_element_type=F32).astype(BF16)
    q_ref[:, aligned:] = keyval[:, :shift]

    @pl.when(jnp.logical_not(has_up))
    def _():
        down_in[...] = jnp.zeros_like(down_in)

    @pl.when(jnp.logical_not(from_diag))
    def _():
        diag_in[...] = jnp.zeros_like(diag_in)

    @pl.when(jnp.logical_not(has_left))
    def _():
        right_in[...] = jnp.zeros_like(right_in)

    pl.when(has_up)(down.wait_recv)
    pl.when(from_diag)(diag.wait_recv)
    pl.when(has_left)(right.wait_recv)

    total = own[...] + down_in[...]
    first_row = lax.broadcasted_iota(jnp.int32, total.shape, 0) == 0
    total = total + jnp.where(first_row, right_in[...] + diag_in[...], 0.0)
    lane = lax.broadcasted_iota(jnp.int32, (1, wide), 1) - shift
    masks = [
        (lane >= at * head_dim) & (lane < (at + 1) * head_dim) for at in range(2 * heads)
    ]

    def head_mean(values):
        result = jnp.zeros_like(values)
        for mask in masks:
            mean = jnp.sum(jnp.where(mask, values, 0.0), axis=-1, keepdims=True) / head_dim
            result = jnp.where(mask, mean, result)
        return result

    def spread_gain(gain_ref, matrix):
        gain = jnp.broadcast_to(gain_ref[...], (8, head_dim))
        return jnp.dot(gain, matrix.astype(F32), precision=lax.Precision.HIGHEST,
                       preferred_element_type=F32)[:1]

    gains = jnp.concatenate(
        [spread_gain(key_gain_ref, key_spread), spread_gain(value_gain_ref, value_spread)], axis=-1)
    centred = total - head_mean(total)
    scaled = centred * lax.rsqrt(head_mean(centred * centred) + EPS) * gains
    me = row * cols_n + col
    blocks[me] = scaled[:, shift:].astype(BF16)

    sends = []

    def send(block, device):
        copy = pltpu.make_async_remote_copy(
            src_ref=blocks.at[block], dst_ref=blocks.at[block],
            send_sem=send_sem.at[len(sends)], recv_sem=recv_sem.at[block],
            device_id=device, device_id_type=MESH)
        copy.start()
        sends.append(copy)

    def arrive(block):
        pltpu.make_async_remote_copy(
            src_ref=blocks.at[block], dst_ref=blocks.at[block],
            send_sem=send_sem.at[0], recv_sem=recv_sem.at[block],
            device_id={"col": lax.rem(col + 1, cols_n)}, device_id_type=MESH).wait_recv()

    def flipped(bit):
        return col + bit - 2 * bit * lax.rem(col // bit, 2)

    bits = []
    bit = cols_n // 2
    while bit >= 1:
        bits.append(bit)
        bit //= 2
    order = [0]
    for step in range(1, rows_n // 2 + 1):
        order += [step] if 2 * step == rows_n else [step, rows_n - step]
    for step in reversed(order[1:]):
        send(me, {"row": lax.rem(row + step, rows_n)})
    have = [col]
    for level in range(len(bits) + 1):
        fresh = have if level == 0 else have[len(have) // 2:]
        for at in fresh:
            for step in order:
                block = lax.rem(row + step, rows_n) * cols_n + at
                if not (level == 0 and step == 0):
                    arrive(block)
                for bit in bits[level:]:
                    send(block, {"col": flipped(bit)})
        if level < len(bits):
            bit = bits[level]
            have = have + [at + bit - 2 * bit * lax.rem(at // bit, 2) for at in have]
    gathered_ref[...] = blocks[...]
    for copy in sends:
        copy.wait_send()
    pl.when(has_down)(down.wait_send)
    pl.when(to_diag)(diag.wait_send)
    pl.when(has_right)(right.wait_send)


def pooled_keys(tokens, w_qkv, pool_kernel, key_gain, value_gain, rows_n, cols_n):
    count, width = tokens.shape
    groups = count // STRIDE // STRIDE
    span = pool_kernel.shape[1]
    shift = width % LANES
    wide = shift + 2 * width
    spaces = rows_n * cols_n
    bits = cols_n.bit_length() - 1
    sends = rows_n - 1 + rows_n * (cols_n - 1)
    vmem = pl.BlockSpec(memory_space=pltpu.VMEM)
    return pl.pallas_call(
        functools.partial(pooled_keys_kernel, rows_n, cols_n, HEADS),
        out_shape=[
            jax.ShapeDtypeStruct((count, width), BF16),
            jax.ShapeDtypeStruct((spaces, groups, 2 * width), BF16),
        ],
        in_specs=[vmem] * 5,
        out_specs=[vmem] * 2,
        scratch_shapes=[
            pltpu.VMEM((count, width), BF16),
            pltpu.VMEM((count, wide), BF16),
            pltpu.VMEM((2, span, STRIDE, wide), F32),
            pltpu.VMEM((groups, wide), F32),
            pltpu.VMEM((spaces, groups, 2 * width), BF16),
            pltpu.VMEM((groups, wide), F32),
            pltpu.VMEM((groups, wide), F32),
            pltpu.VMEM((1, wide), F32),
            pltpu.VMEM((1, wide), F32),
            pltpu.VMEM((1, wide), F32),
            pltpu.VMEM((1, wide), F32),
            pltpu.SemaphoreType.DMA((3,)),
            pltpu.SemaphoreType.DMA((3,)),
            pltpu.SemaphoreType.DMA((sends,)),
            pltpu.SemaphoreType.DMA((spaces,)),
        ],
        compiler_params=pltpu.CompilerParams(
            collective_id=0, has_side_effects=True, vmem_limit_bytes=36 * 2**20),
        cost_estimate=pl.CostEstimate(
            flops=2 * count * width * 3 * width, bytes_accessed=6 * 2**20, transcendentals=0),
        name="pooled_keys",
    )(tokens, w_qkv, pool_kernel, key_gain.reshape(1, -1), value_gain.reshape(1, -1))


def windows(width, heads):
    head_dim = width // heads
    result = []
    for head in range(0, heads, 2):
        start = head * head_dim // LANES * LANES
        stop = min(-(-(head + 2) * head_dim // LANES) * LANES, width)
        result.append((start, stop, head * head_dim - start))
    return result


def finish_kernel(heads, q_ref, tokens_ref, pooled_ref, w_proj_ref, w_up_ref, w_down_ref,
                  out_ref, keys, values):
    rows, width = q_ref.shape
    head_dim = width // heads
    spots = pooled_ref.shape[0]
    places = windows(width, heads)

    @pl.when(pl.program_id(0) == 0)
    def _():
        all_keys = pooled_ref[:, :width]
        all_values = pooled_ref[:, width:]
        for pair, (start, stop, at) in enumerate(places):
            lane = lax.broadcasted_iota(jnp.int32, (spots, stop - start), 1)
            for side in range(2):
                first = at + side * head_dim
                mask = (lane >= first) & (lane < first + head_dim)
                spot = pl.ds(side * spots, spots)
                keys[pair, spot, :stop - start] = jnp.where(
                    mask, all_keys[:, start:stop].astype(F32), 0.0).astype(BF16)
                values[pair, spot, :stop - start] = jnp.where(
                    mask, all_values[:, start:stop].astype(F32), 0.0).astype(BF16)

    factor = head_dim ** -0.5 * math.log2(math.e)
    tiles = [None] * (-(-width // LANES))
    for pair, (start, stop, at) in enumerate(places):
        size = stop - start
        scores = lax.dot_general(
            q_ref[:, start:stop], keys[pair, :, :size], (((1,), (1,)), ((), ())),
            preferred_element_type=F32)
        probs, scales = [], []
        for side in range(2):
            part = scores[:, side * spots:(side + 1) * spots]
            top = jnp.max(part, axis=-1, keepdims=True)
            weights = jnp.exp2((part - top) * factor)
            scales.append(1.0 / jnp.sum(weights, axis=-1, keepdims=True))
            probs.append(weights.astype(BF16))
        mixed = jnp.dot(jnp.concatenate(probs, axis=-1), values[pair, :, :size],
                        preferred_element_type=F32)
        lane = lax.broadcasted_iota(jnp.int32, (1, size), 1)
        mixed = mixed * jnp.where(lane < at + head_dim, scales[0], scales[1])
        for tile in range(0, size, LANES):
            piece = mixed[:, tile:tile + LANES]
            index = (start + tile) // LANES
            tiles[index] = piece if tiles[index] is None else tiles[index] + piece
    attended = (jnp.concatenate(tiles, axis=-1) + q_ref[...].astype(F32)).astype(BF16)
    residual = (
        tokens_ref[...].astype(F32)
        + jnp.dot(attended, w_proj_ref[...], preferred_element_type=F32)
    ).astype(BF16)
    residual = residual.astype(F32)
    renormed = layer_norm(residual).astype(BF16)
    ffn = w_up_ref.shape[1]
    chunk = math.gcd(ffn, 768)
    total = residual
    for start in range(0, ffn, chunk):
        hidden = jnp.dot(renormed, w_up_ref[:, start:start + chunk], preferred_element_type=F32)
        active = (hidden * (0.5 + 0.5 * lax.erf(hidden * (0.5 ** 0.5)))).astype(BF16)
        total = total + jnp.dot(active, w_down_ref[start:start + chunk, :],
                                preferred_element_type=F32)
    out_ref[...] = total.astype(BF16)


def finish(query, tokens, pooled, w_proj, w_up, w_down):
    count, width = query.shape
    spots = pooled.shape[0]
    rows = math.gcd(count, 256 if spots <= 512 else 128)
    block = pl.BlockSpec((rows, width), lambda i: (i, 0))
    vmem = pl.BlockSpec(memory_space=pltpu.VMEM)
    places = windows(width, HEADS)
    size = max(stop - start for start, stop, _ in places)
    ffn = w_up.shape[1]
    return pl.pallas_call(
        functools.partial(finish_kernel, HEADS),
        grid=(count // rows,),
        out_shape=jax.ShapeDtypeStruct((count, width), BF16),
        in_specs=[block, block, vmem, vmem, vmem, vmem],
        out_specs=block,
        scratch_shapes=[
            pltpu.VMEM((len(places), 2 * spots, size), BF16),
            pltpu.VMEM((len(places), 2 * spots, size), BF16),
        ],
        compiler_params=pltpu.CompilerParams(vmem_limit_bytes=52 * 2**20),
        cost_estimate=pl.CostEstimate(
            flops=2 * count * width * (width + 2 * ffn + 2 * spots),
            bytes_accessed=10 * 2**20, transcendentals=count * (ffn + HEADS * spots)),
        name="finish",
    )(query, tokens, pooled, w_proj, w_up, w_down)


def per_device(rows_n, cols_n, tokens, w_qkv, pool_kernel, key_gain, value_gain, w_proj, w_up,
               w_down):
    rows, cols, width = tokens.shape
    flat = tokens.reshape(rows * cols, width)
    query, pooled = pooled_keys(flat, w_qkv, pool_kernel, key_gain, value_gain, rows_n, cols_n)
    result = finish(query, flat, pooled.reshape(-1, 2 * width), w_proj, w_up, w_down)
    return result.reshape(rows, cols, width)


def solution(mesh):
    in_specs = (P(("maps", "row"), "col", None), P(), P(), P(), P(), P(), P(), P())
    out_specs = P(("maps", "row"), "col", None)
    body = functools.partial(per_device, mesh.shape["row"], mesh.shape["col"])
    return jax.shard_map(
        body, mesh=mesh, in_specs=in_specs, out_specs=out_specs, check_vma=False
    )
```

time: 266 us -> 49.7 us (0.19)
  matrix products: 172 us -> 0 us
  Pallas kernels: 0 us -> 37.9 us
  blocking collectives: 25.1 us -> 0 us
  local copies, waits for them, and re-layouts: 36.4 us -> 11.6 us
  waiting for transfers between devices: 13.2 us -> 0 us
  other arithmetic: 9.83 us -> 0 us
  starting transfers between devices: 7.86 us -> 0 us
    conv_general_dilated x1 -> x0, matrix products: 131 us -> none  [pool(): lax.conv_general_dilated(framed[None], full, (stride, stride), pads, dime...]
    dot_general x9 -> x0, matrix products: 40.8 us -> none  [the longest x2 31.6 us: finish_block(): jnp.dot(hidden_act, w_down, preferred_element_type=jnp.float32)]
    pallas_call x0 -> x2, Pallas kernels: none -> 37.9 us  [the longest x1 19.3 us: pooled_keys(): pl.pallas_call(functools.partial(pooled_keys_kernel, rows_n, cols_n, HEAD...]
    all_gather x1 -> x0, blocking collectives: 25.1 us -> none  [per_device(): gathered = lax.all_gather(pooled_kv, ('row', 'col'), axis=0, tiled=True)]
    ppermute x2 -> x0, waiting for transfers between devices: 13.2 us -> none  [from_behind(): return lax.ppermute(block, axis, route)]
    ppermute x2 -> x0, starting transfers between devices: 7.86 us -> none  [from_behind(): return lax.ppermute(block, axis, route)]
    another operation x7 -> x0, local copies, waits for them, and re-layouts: 7.22 us -> none  [the longest x1 2.75 us: per_device(): flat.reshape(count // block, block, width)]
    unnamed x17 -> x19, local copies, waits for them, and re-layouts: 3.66 us -> 9.16 us
  transfers between devices with their start and end apart: 2 -> 0, of which waited for: 2 -> 0; matrix products, arithmetic and copies ran while one was open for 5% -> 0% of each run, Pallas kernels for 0% -> 0%
where the time goes in v1:
time: 49.7 us; the launch traced here: 49.5 us
  Pallas kernels  37.9 us (76%)
  local copies, waits for them, and re-layouts  11.6 us (23%)
    pallas_call x1, Pallas kernels, pooled_keys(): pl.pallas_call(functools.partial(pooled_keys_kernel, rows_n, cols_n, HEAD...  19.3 us
    pallas_call x1, Pallas kernels, finish(): pl.pallas_call(functools.partial(finish_kernel, HEADS), grid=(count // ro...  18.6 us
    unnamed x19, local copies, waits for them, and re-layouts  9.16 us
    reshape x1, local copies, waits for them, and re-layouts, per_device(): return result.reshape(rows, cols, width)  2.39 us

profile of v1, /device:TPU:0, one launch (start us, length us, event | category | flops | bytes accessed | tf_op | source)
XLA Modules:
  0.0 49.5 jit_solution(5010304208192772643)
XLA Ops:
  0.0 0.0 copy-start.4
  0.0 0.0 copy-start.3
  0.0 0.0 copy-start.1
  0.0 0.9 %copy.10.pool_ref = bf16[2,9,9,72]{3,2,1,0:T(8,128)(2,1)S(1)} copy(bf16[2,9,9,72]{3,0,2,1:T(2,128)(2,1)} %param.10) | data formatting | bytes 46656 | tf_op args[2]
  0.9 1.7 %copy.9 = bf16[8,128,576]{2,1,0:T(8,128)(2,1)S(1)} copy(bf16[8,128,576]{1,2,0:T(8,128)(2,1)} %param.8) | data formatting | bytes 2359296 | tf_op args[0]
  2.6 0.0 copy-start
  2.6 0.0 copy-done.4
  2.7 0.0 copy-done.3
  2.7 0.0 copy-done.1
  2.7 19.3 %pooled_keys.1 = (bf16[1024,576]{1,0:T(8,128)(2,1)S(1)}, bf16[16,16,1152]{2,1,0:T(8,128)(2,1)S(1)}) custom-call(bf16[1024,576]{1,0:T(8,128)(2,1)S(1)} %bitcast.5, bf16[576,1728]{1,0:T(8,128)(2,1)S(1)} %copy-done.1, bf16[2,9,9,72]{3,2,1,0:T(8,128)(2,1)S(1)} %copy.10.pool_ref, f32[1,72]{1,0:T(1,128)S(1)} %bitcast.7, f32[1,72]{1,0:T(1,128)S(1)} %bitcast.8), custom_call_target="tpu_custom_call" | custom-call | flops 2038431744 | bytes 6291456 | tf_op jit(solution)/shard_map/pooled_keys/pallas_call | solution.py:242
  22.0 0.0 copy-done
  22.0 0.0 copy-start.5
  22.0 0.8 %copy-done.5 = bf16[16,16,1152]{2,1,0:T(8,128)(2,1)} copy-done((bf16[16,16,1152]{2,1,0:T(8,128)(2,1)}, bf16[16,16,1152]{2,1,0:T(8,128)(2,1)S(1)}, u32[]{:S(2)}) %copy-start.5) | copy-done | bytes 589848
  22.8 0.0 copy-start.7
  22.8 1.1 %copy-done.7 = bf16[1024,576]{1,0:T(8,128)(2,1)} copy-done((bf16[1024,576]{1,0:T(8,128)(2,1)}, bf16[1024,576]{1,0:T(8,128)(2,1)S(1)}, u32[]{:S(2)}) %copy-start.7) | copy-done | bytes 1179672
  23.9 0.0 copy-start.2
  23.9 0.0 copy-start.6
  23.9 4.6 %copy.11.w_down_ref = bf16[2304,576]{1,0:T(8,128)(2,1)} copy(bf16[2304,576]{0,1:T(8,128)(2,1)} %param.15) | data formatting | bytes 5308416 | tf_op args[7]
  28.5 0.0 copy-done.2
  28.5 0.0 copy-done.6
  28.5 18.6 %finish.1 = bf16[1024,576]{1,0:T(8,128)(2,1)} custom-call(bf16[1024,576]{1,0:T(8,128)(2,1)} %copy-done.7, bf16[1024,576]{1,0:T(8,128)(2,1)} %bitcast.6, bf16[256,1152]{1,0:T(8,128)(2,1)S(1)} %bitcast.9, bf16[576,576]{1,0:T(8,128)(2,1)S(1)} %copy-done.2, bf16[576,2304]{1,0:T(8,128)(2,1)} %w_up_ref.1, bf16[2304,576]{1,0:T(8,128)(2,1)} %copy.11.w_down_ref), custom_call_target="tpu_custom_call" | custom-call | flops 6719275008 | bytes 10485760 | tf_op jit(solution)/shard_map/finish/pallas_call | solution.py:356
  47.1 2.4 %copy.12 = bf16[8,128,576]{1,2,0:T(8,128)(2,1)} copy(bf16[8,128,576]{2,1,0:T(8,128)(2,1)} %bitcast.10) | data formatting | bytes 2359296 | tf_op jit(solution)/shard_map/reshape | solution.py:380
Async XLA Ops:
  0.0 2.6 %copy-start.4 = (f32[72]{0:T(128)S(1)}, f32[72]{0:T(128)}, u32[]{:S(2)}) copy-start(f32[72]{0:T(128)} %param.12) | copy-start | bytes 868
  0.0 2.7 %copy-start.3 = (f32[72]{0:T(128)S(1)}, f32[72]{0:T(128)}, u32[]{:S(2)}) copy-start(f32[72]{0:T(128)} %param.11) | copy-start | bytes 868
  0.0 2.7 %copy-start.1 = (bf16[576,1728]{1,0:T(8,128)(2,1)S(1)}, bf16[576,1728]{1,0:T(8,128)(2,1)}, u32[]{:S(2)}) copy-start(bf16[576,1728]{1,0:T(8,128)(2,1)} %w_ref.1) | copy-start | bytes 5971972
  2.6 19.3 %copy-start = (bf16[8,128,576]{2,1,0:T(8,128)(2,1)}, bf16[8,128,576]{2,1,0:T(8,128)(2,1)S(1)}, u32[]{:S(2)}) copy-start(bf16[8,128,576]{2,1,0:T(8,128)(2,1)S(1)} %copy.9) | copy-start | bytes 3538948
  22.0 0.8 %copy-start.5 = (bf16[16,16,1152]{2,1,0:T(8,128)(2,1)}, bf16[16,16,1152]{2,1,0:T(8,128)(2,1)S(1)}, u32[]{:S(2)}) copy-start(bf16[16,16,1152]{2,1,0:T(8,128)(2,1)S(1)} %get-tuple-element.8) | copy-start | bytes 1769476
  22.8 1.1 %copy-start.7 = (bf16[1024,576]{1,0:T(8,128)(2,1)}, bf16[1024,576]{1,0:T(8,128)(2,1)S(1)}, u32[]{:S(2)}) copy-start(bf16[1024,576]{1,0:T(8,128)(2,1)S(1)} %get-tuple-element.7.q_ref) | copy-start | bytes 3538948
  23.9 4.6 %copy-start.2 = (bf16[576,576]{1,0:T(8,128)(2,1)S(1)}, bf16[576,576]{1,0:T(8,128)(2,1)}, u32[]{:S(2)}) copy-start(bf16[576,576]{1,0:T(8,128)(2,1)} %w_proj_ref.1) | copy-start | bytes 1990660
  23.9 4.6 %copy-start.6 = (bf16[16,16,1152]{2,1,0:T(8,128)(2,1)S(1)}, bf16[16,16,1152]{2,1,0:T(8,128)(2,1)}, u32[]{:S(2)}) copy-start(bf16[16,16,1152]{2,1,0:T(8,128)(2,1)} %copy-done.5) | copy-start | bytes 1769476

commit v2 on v1

--- a/solution.py
+++ b/solution.py
@@ -17,10 +17,10 @@
 BF16 = jnp.bfloat16
 
 
-def layer_norm(values):
-    mean = jnp.mean(values, axis=-1, keepdims=True)
+def layer_norm(values, axis):
+    mean = jnp.mean(values, axis=axis, keepdims=True)
     centred = values - mean
-    spread = jnp.mean(centred * centred, axis=-1, keepdims=True)
+    spread = jnp.mean(centred * centred, axis=axis, keepdims=True)
     return centred * lax.rsqrt(spread + EPS)
 
 
@@ -41,11 +41,10 @@
     down_out, down_in, diag_out, diag_in, right_out, right_in,
     halo_send, halo_recv, send_sem, recv_sem,
 ):
-    count, width = tokens_ref.shape
+    _, width, cols = tokens_ref.shape
     head_dim = width // heads
-    cols = count // STRIDE
     groups = cols // STRIDE
-    span = pool_ref.shape[1]
+    span = pool_ref.shape[0]
     reach = span // 2
     aligned = width // LANES * LANES
     shift = width - aligned
@@ -76,14 +75,17 @@
 
     key_spread = spread_matrix(head_dim, shift + width, heads, shift, BF16)
     value_spread = spread_matrix(head_dim, width, heads, 0, BF16)
+    def spread_taps(side, matrix):
+        room = jnp.zeros((16 - span, head_dim), F32)
+        lines = []
+        for a in range(span):
+            lines += [pool_ref[a].astype(F32)[:, side, :], room]
+        lines = jnp.concatenate(lines, axis=0).astype(BF16)
+        return jnp.dot(lines, matrix, preferred_element_type=F32)
+
+    spread = jnp.concatenate([spread_taps(0, key_spread), spread_taps(1, value_spread)], axis=-1)
     for a in range(span):
-        line = jnp.concatenate(
-            [
-                jnp.dot(pool_ref[0, a], key_spread, preferred_element_type=F32),
-                jnp.dot(pool_ref[1, a], value_spread, preferred_element_type=F32),
-            ],
-            axis=-1,
-        )
+        line = spread[16 * a:16 * a + span]
         below = jnp.zeros((STRIDE - reach - 1, wide), F32)
         above = jnp.zeros((STRIDE - reach, wide), F32)
         taps[0, a] = jnp.concatenate([line[reach:], below], axis=0)
@@ -92,7 +94,8 @@
     def project(first, last):
         for at in range(first, last):
             line = pl.ds(at * cols, cols)
-            normed[line, :] = layer_norm(tokens_ref[line, :].astype(F32)).astype(BF16)
+            normed[line, :] = jnp.transpose(
+                layer_norm(tokens_ref[at].astype(F32), 0).astype(BF16))
         part = pl.ds(first * cols, (last - first) * cols)
         keyval[part, :] = jnp.dot(
             normed[part, :], w_ref[:, aligned:], preferred_element_type=F32).astype(BF16)
@@ -230,13 +233,13 @@
 
 
 def pooled_keys(tokens, w_qkv, pool_kernel, key_gain, value_gain, rows_n, cols_n):
-    count, width = tokens.shape
-    groups = count // STRIDE // STRIDE
-    span = pool_kernel.shape[1]
+    rows, width, cols = tokens.shape
+    count = rows * cols
+    groups = cols // STRIDE
+    span = pool_kernel.shape[0]
     shift = width % LANES
     wide = shift + 2 * width
     spaces = rows_n * cols_n
-    bits = cols_n.bit_length() - 1
     sends = rows_n - 1 + rows_n * (cols_n - 1)
     vmem = pl.BlockSpec(memory_space=pltpu.VMEM)
     return pl.pallas_call(
@@ -265,7 +268,7 @@
             pltpu.SemaphoreType.DMA((spaces,)),
         ],
         compiler_params=pltpu.CompilerParams(
-            collective_id=0, has_side_effects=True, vmem_limit_bytes=36 * 2**20),
+            collective_id=0, has_side_effects=True, vmem_limit_bytes=(20 if spaces <= 16 else 40) * 2**20),
         cost_estimate=pl.CostEstimate(
             flops=2 * count * width * 3 * width, bytes_accessed=6 * 2**20, transcendentals=0),
         name="pooled_keys",
@@ -280,6 +283,16 @@
         stop = min(-(-(head + 2) * head_dim // LANES) * LANES, width)
         result.append((start, stop, head * head_dim - start))
     return result
+
+
+def gelu(x):
+    size = jnp.abs(x)
+    t = pl.reciprocal(1.0 + (0.3275911 * 0.5 ** 0.5) * size, approx=False)
+    tail = 0.5 * 1.061405429
+    for term in (-1.453152027, 1.421413741, -0.284496736, 0.254829592):
+        tail = tail * t + 0.5 * term
+    tail = tail * t * jnp.exp2(x * x * (-0.5 * math.log2(math.e)))
+    return jnp.maximum(x, 0.0) - size * tail
 
 
 def finish_kernel(heads, q_ref, tokens_ref, pooled_ref, w_proj_ref, w_up_ref, w_down_ref,
@@ -327,43 +340,49 @@
             index = (start + tile) // LANES
             tiles[index] = piece if tiles[index] is None else tiles[index] + piece
     attended = (jnp.concatenate(tiles, axis=-1) + q_ref[...].astype(F32)).astype(BF16)
+    tokens = jnp.concatenate(
+        [jnp.transpose(tokens_ref[at]) for at in range(tokens_ref.shape[0])], axis=0)
     residual = (
-        tokens_ref[...].astype(F32)
+        tokens.astype(F32)
         + jnp.dot(attended, w_proj_ref[...], preferred_element_type=F32)
     ).astype(BF16)
-    residual = residual.astype(F32)
-    renormed = layer_norm(residual).astype(BF16)
+    renormed = layer_norm(residual.astype(F32), -1).astype(BF16)
     ffn = w_up_ref.shape[1]
     chunk = math.gcd(ffn, 768)
-    total = residual
+    total = jnp.transpose(residual).astype(F32)
     for start in range(0, ffn, chunk):
         hidden = jnp.dot(renormed, w_up_ref[:, start:start + chunk], preferred_element_type=F32)
-        active = (hidden * (0.5 + 0.5 * lax.erf(hidden * (0.5 ** 0.5)))).astype(BF16)
-        total = total + jnp.dot(active, w_down_ref[start:start + chunk, :],
-                                preferred_element_type=F32)
-    out_ref[...] = total.astype(BF16)
+        total = total + lax.dot_general(
+            w_down_ref[:, start:start + chunk], gelu(hidden).astype(BF16),
+            (((1,), (1,)), ((), ())), preferred_element_type=F32)
+    total = total.astype(BF16)
+    cols = tokens_ref.shape[-1]
+    for at in range(tokens_ref.shape[0]):
+        out_ref[at] = total[:, at * cols:(at + 1) * cols]
 
 
 def finish(query, tokens, pooled, w_proj, w_up, w_down):
     count, width = query.shape
     spots = pooled.shape[0]
-    rows = math.gcd(count, 256 if spots <= 512 else 128)
-    block = pl.BlockSpec((rows, width), lambda i: (i, 0))
+    cols = tokens.shape[-1]
+    lines = math.gcd(count // cols, 2 if spots <= 512 else 1)
+    block = pl.BlockSpec((lines * cols, width), lambda i: (i, 0))
+    turned = pl.BlockSpec((lines, width, cols), lambda i: (i, 0, 0))
     vmem = pl.BlockSpec(memory_space=pltpu.VMEM)
     places = windows(width, HEADS)
     size = max(stop - start for start, stop, _ in places)
     ffn = w_up.shape[1]
     return pl.pallas_call(
         functools.partial(finish_kernel, HEADS),
-        grid=(count // rows,),
-        out_shape=jax.ShapeDtypeStruct((count, width), BF16),
-        in_specs=[block, block, vmem, vmem, vmem, vmem],
-        out_specs=block,
+        grid=(count // cols // lines,),
+        out_shape=jax.ShapeDtypeStruct(tokens.shape, BF16),
+        in_specs=[block, turned, vmem, vmem, vmem, vmem],
+        out_specs=turned,
         scratch_shapes=[
             pltpu.VMEM((len(places), 2 * spots, size), BF16),
             pltpu.VMEM((len(places), 2 * spots, size), BF16),
         ],
-        compiler_params=pltpu.CompilerParams(vmem_limit_bytes=52 * 2**20),
+        compiler_params=pltpu.CompilerParams(vmem_limit_bytes=(24 if spots <= 512 else 52) * 2**20),
         cost_estimate=pl.CostEstimate(
             flops=2 * count * width * (width + 2 * ffn + 2 * spots),
             bytes_accessed=10 * 2**20, transcendentals=count * (ffn + HEADS * spots)),
@@ -373,11 +392,12 @@
 
 def per_device(rows_n, cols_n, tokens, w_qkv, pool_kernel, key_gain, value_gain, w_proj, w_up,
                w_down):
-    rows, cols, width = tokens.shape
-    flat = tokens.reshape(rows * cols, width)
-    query, pooled = pooled_keys(flat, w_qkv, pool_kernel, key_gain, value_gain, rows_n, cols_n)
-    result = finish(query, flat, pooled.reshape(-1, 2 * width), w_proj, w_up, w_down)
-    return result.reshape(rows, cols, width)
+    turned = jnp.swapaxes(tokens, 1, 2)
+    query, pooled = pooled_keys(
+        turned, w_qkv, jnp.transpose(pool_kernel, (1, 2, 0, 3)), key_gain, value_gain,
+        rows_n, cols_n)
+    result = finish(query, turned, pooled.reshape(-1, pooled.shape[-1]), w_proj, w_up, w_down.T)
+    return jnp.swapaxes(result, 1, 2)
 
 
 def solution(mesh):

time: 49.7 us -> 43.2 us (0.87)
  local copies, waits for them, and re-layouts: 11.6 us -> 4.95 us
    unnamed x19 -> x18, local copies, waits for them, and re-layouts: 9.16 us -> 4.95 us
    reshape x1 -> x0, local copies, waits for them, and re-layouts: 2.39 us -> none  [per_device(): return result.reshape(rows, cols, width)]
where the time goes in v2:
time: 43.2 us; the launch traced here: 42.9 us
  Pallas kernels  37.9 us (88%)
  local copies, waits for them, and re-layouts  4.95 us (11%)
    pallas_call x1, Pallas kernels, pooled_keys(): pl.pallas_call(functools.partial(pooled_keys_kernel, rows_n, cols_n, HEAD...  19.4 us
    pallas_call x1, Pallas kernels, finish(): pl.pallas_call(functools.partial(finish_kernel, HEADS), grid=(count // co...  18.5 us
    unnamed x18, local copies, waits for them, and re-layouts  4.95 us

profile of v2, /device:TPU:0, one launch (start us, length us, event | category | flops | bytes accessed | tf_op | source)
XLA Modules:
  0.0 42.9 jit_solution(414547938673756762)
XLA Ops:
  0.0 0.0 copy-start.2
  0.0 1.6 %copy-done.2 = bf16[576,1728]{1,0:T(8,128)(2,1)S(1)} copy-done((bf16[576,1728]{1,0:T(8,128)(2,1)S(1)}, bf16[576,1728]{1,0:T(8,128)(2,1)}, u32[]{:S(2)}) %copy-start.2) | copy-done | bytes 1990680
  1.6 0.0 copy-start.3
  1.6 1.3 %copy-done.3 = bf16[8,128,576]{1,2,0:T(8,128)(2,1)S(1)} copy-done((bf16[8,128,576]{1,2,0:T(8,128)(2,1)S(1)}, bf16[8,128,576]{1,2,0:T(8,128)(2,1)}, u32[]{:S(2)}) %copy-start.3) | copy-done | bytes 1179672
  2.9 0.0 copy-start.6
  2.9 0.8 %copy-done.6 = bf16[2,9,9,72]{3,0,2,1:T(2,128)(2,1)S(1)} copy-done((bf16[2,9,9,72]{3,0,2,1:T(2,128)(2,1)S(1)}, bf16[2,9,9,72]{3,0,2,1:T(2,128)(2,1)}, u32[]{:S(2)}) %copy-start.6) | copy-done | bytes 23352
  3.6 0.0 copy-start.7
  3.6 0.7 %copy-done.7 = f32[72]{0:T(128)S(1)} copy-done((f32[72]{0:T(128)S(1)}, f32[72]{0:T(128)}, u32[]{:S(2)}) %copy-start.7) | copy-done | bytes 312
  4.3 0.0 copy-start.8
  4.3 0.7 %copy-done.8 = f32[72]{0:T(128)S(1)} copy-done((f32[72]{0:T(128)S(1)}, f32[72]{0:T(128)}, u32[]{:S(2)}) %copy-start.8) | copy-done | bytes 312
  4.9 0.0 copy-start
  4.9 0.0 copy-start.1
  4.9 0.0 copy-start.4
  4.9 0.0 copy-start.5
  5.0 19.4 %pooled_keys.1 = (bf16[1024,576]{1,0:T(8,128)(2,1)S(1)}, bf16[16,16,1152]{2,1,0:T(8,128)(2,1)S(1)}) custom-call(bf16[8,576,128]{2,1,0:T(8,128)(2,1)S(1)} %bitcast.8, bf16[576,1728]{1,0:T(8,128)(2,1)S(1)} %copy-done.2, bf16[9,9,2,72]{3,2,1,0:T(2,128)(2,1)S(1)} %bitcast.10, f32[1,72]{1,0:T(1,128)S(1)} %bitcast.11, f32[1,72]{1,0:T(1,128)S(1)} %bitcast.12), custom_call_target="tpu_custom_call" | custom-call | flops 2038431744 | bytes 6291456 | tf_op jit(solution)/shard_map/pooled_keys/pallas_call | solution.py:245
  24.4 0.0 copy-done
  24.4 0.0 copy-done.1
  24.4 0.0 copy-done.4
  24.4 0.0 copy-done.5
  24.4 18.5 %finish.1 = bf16[8,576,128]{2,1,0:T(8,128)(2,1)} custom-call(bf16[1024,576]{1,0:T(8,128)(2,1)S(1)} %get-tuple-element.7.q_ref, bf16[8,576,128]{2,1,0:T(8,128)(2,1)S(1)} %bitcast.9, bf16[256,1152]{1,0:T(8,128)(2,1)S(1)} %bitcast.13, bf16[576,576]{1,0:T(8,128)(2,1)S(1)} %copy-done.5, bf16[576,2304]{1,0:T(8,128)(2,1)S(1)} %copy-done, bf16[576,2304]{1,0:T(8,128)(2,1)S(1)} %bitcast.7), custom_call_target="tpu_custom_call" | custom-call | flops 6719275008 | bytes 10485760 | tf_op jit(solution)/shard_map/finish/pallas_call | solution.py:375
Async XLA Ops:
  0.0 1.6 %copy-start.2 = (bf16[576,1728]{1,0:T(8,128)(2,1)S(1)}, bf16[576,1728]{1,0:T(8,128)(2,1)}, u32[]{:S(2)}) copy-start(bf16[576,1728]{1,0:T(8,128)(2,1)} %w_ref.1) | copy-start | bytes 5971972
  1.6 1.3 %copy-start.3 = (bf16[8,128,576]{1,2,0:T(8,128)(2,1)S(1)}, bf16[8,128,576]{1,2,0:T(8,128)(2,1)}, u32[]{:S(2)}) copy-start(bf16[8,128,576]{1,2,0:T(8,128)(2,1)} %param.8) | copy-start | bytes 3538948
  2.9 0.8 %copy-start.6 = (bf16[2,9,9,72]{3,0,2,1:T(2,128)(2,1)S(1)}, bf16[2,9,9,72]{3,0,2,1:T(2,128)(2,1)}, u32[]{:S(2)}) copy-start(bf16[2,9,9,72]{3,0,2,1:T(2,128)(2,1)} %param.10) | copy-start | bytes 69988
  3.6 0.7 %copy-start.7 = (f32[72]{0:T(128)S(1)}, f32[72]{0:T(128)}, u32[]{:S(2)}) copy-start(f32[72]{0:T(128)} %param.11) | copy-start | bytes 868
  4.3 0.7 %copy-start.8 = (f32[72]{0:T(128)S(1)}, f32[72]{0:T(128)}, u32[]{:S(2)}) copy-start(f32[72]{0:T(128)} %param.12) | copy-start | bytes 868
  4.9 19.4 %copy-start = (bf16[576,2304]{1,0:T(8,128)(2,1)S(1)}, bf16[576,2304]{1,0:T(8,128)(2,1)}, u32[]{:S(2)}) copy-start(bf16[576,2304]{1,0:T(8,128)(2,1)} %w_up_ref.1) | copy-start | bytes 7962628
  4.9 19.4 %copy-start.1 = (bf16[2304,576]{0,1:T(8,128)(2,1)S(1)}, bf16[2304,576]{0,1:T(8,128)(2,1)}, u32[]{:S(2)}) copy-start(bf16[2304,576]{0,1:T(8,128)(2,1)} %param.15) | copy-start | bytes 7962628
  4.9 19.5 %copy-start.4 = (bf16[8,128,576]{1,2,0:T(8,128)(2,1)S(1)}, bf16[8,128,576]{1,2,0:T(8,128)(2,1)}, u32[]{:S(2)}) copy-start(bf16[8,128,576]{1,2,0:T(8,128)(2,1)} %param.8) | copy-start | bytes 3538948
  4.9 19.5 %copy-start.5 = (bf16[576,576]{1,0:T(8,128)(2,1)S(1)}, bf16[576,576]{1,0:T(8,128)(2,1)}, u32[]{:S(2)}) copy-start(bf16[576,576]{1,0:T(8,128)(2,1)} %w_proj_ref.1) | copy-start | bytes 1990660

commit v3 on v2

--- a/solution.py
+++ b/solution.py
@@ -35,8 +35,9 @@
 
 def pooled_keys_kernel(
     rows_n, cols_n, heads,
-    tokens_ref, w_ref, pool_ref, key_gain_ref, value_gain_ref,
-    q_ref, gathered_ref,
+    tokens_hbm, w_hbm, pool_ref, key_gain_hbm, value_gain_hbm,
+    q_hbm, gathered_ref,
+    q_ref, q_sem, tokens_ref, w_ref, key_gain_ref, value_gain_ref, load_sem,
     normed, keyval, taps, own, blocks,
     down_out, down_in, diag_out, diag_in, right_out, right_in,
     halo_send, halo_recv, send_sem, recv_sem,
@@ -55,6 +56,19 @@
     to_diag = jnp.logical_and(has_down, has_right)
     from_diag = jnp.logical_and(has_up, has_left)
 
+    loads = []
+    for source, target, place in (
+        (tokens_hbm, tokens_ref, (pl.ds(reach, STRIDE - reach),)),
+        (w_hbm, w_ref, (slice(None), pl.ds(aligned, wide))),
+        (tokens_hbm, tokens_ref, (pl.ds(0, reach),)),
+        (w_hbm, w_ref, (slice(None), pl.ds(0, aligned))),
+        (key_gain_hbm, key_gain_ref, (slice(None),)),
+        (value_gain_hbm, value_gain_ref, (slice(None),)),
+    ):
+        loads.append(pltpu.make_async_copy(
+            source.at[place], target.at[place], load_sem.at[len(loads)]))
+        loads[-1].start()
+
     barrier = pltpu.get_barrier_semaphore()
     for step in range(1, rows_n):
         pl.semaphore_signal(
@@ -125,19 +139,25 @@
                 {"row": lax.rem(row + 1, rows_n), "col": lax.rem(col + 1, cols_n)})
     right = halo(2, right_out, right_in, {"col": lax.rem(col + 1, cols_n)})
 
+    loads[0].wait()
+    loads[1].wait()
     project(reach, STRIDE)
     pool(reach, STRIDE, -reach, down_out, diag_out)
     pl.semaphore_wait(
         barrier, rows_n - 1 + cols_n - 1 + to_diag.astype(jnp.int32) + from_diag.astype(jnp.int32))
     pl.when(has_down)(down.start)
     pl.when(to_diag)(diag.start)
+    loads[2].wait()
     project(0, reach)
     pool(0, reach + 1, reach, own, right_out)
     pl.when(has_right)(right.start)
 
+    loads[3].wait()
     q_ref[:, :aligned] = jnp.dot(
         normed[...], w_ref[:, :aligned], preferred_element_type=F32).astype(BF16)
     q_ref[:, aligned:] = keyval[:, :shift]
+    q_store = pltpu.make_async_copy(q_ref, q_hbm, q_sem)
+    q_store.start()
 
     @pl.when(jnp.logical_not(has_up))
     def _():
@@ -175,6 +195,8 @@
         return jnp.dot(gain, matrix.astype(F32), precision=lax.Precision.HIGHEST,
                        preferred_element_type=F32)[:1]
 
+    loads[4].wait()
+    loads[5].wait()
     gains = jnp.concatenate(
         [spread_gain(key_gain_ref, key_spread), spread_gain(value_gain_ref, value_spread)], axis=-1)
     centred = total - head_mean(total)
@@ -225,6 +247,7 @@
             bit = bits[level]
             have = have + [at + bit - 2 * bit * lax.rem(at // bit, 2) for at in have]
     gathered_ref[...] = blocks[...]
+    q_store.wait()
     for copy in sends:
         copy.wait_send()
     pl.when(has_down)(down.wait_send)
@@ -242,15 +265,23 @@
     spaces = rows_n * cols_n
     sends = rows_n - 1 + rows_n * (cols_n - 1)
     vmem = pl.BlockSpec(memory_space=pltpu.VMEM)
+    hbm = pl.BlockSpec(memory_space=pltpu.HBM)
     return pl.pallas_call(
         functools.partial(pooled_keys_kernel, rows_n, cols_n, HEADS),
         out_shape=[
             jax.ShapeDtypeStruct((count, width), BF16),
             jax.ShapeDtypeStruct((spaces, groups, 2 * width), BF16),
         ],
-        in_specs=[vmem] * 5,
-        out_specs=[vmem] * 2,
+        in_specs=[hbm, hbm, vmem, hbm, hbm],
+        out_specs=[hbm, vmem],
         scratch_shapes=[
+            pltpu.VMEM((count, width), BF16),
+            pltpu.SemaphoreType.DMA,
+            pltpu.VMEM(tokens.shape, BF16),
+            pltpu.VMEM(w_qkv.shape, BF16),
+            pltpu.VMEM((1, key_gain.shape[0]), F32),
+            pltpu.VMEM((1, value_gain.shape[0]), F32),
+            pltpu.SemaphoreType.DMA((6,)),
             pltpu.VMEM((count, width), BF16),
             pltpu.VMEM((count, wide), BF16),
             pltpu.VMEM((2, span, STRIDE, wide), F32),
@@ -268,7 +299,7 @@
             pltpu.SemaphoreType.DMA((spaces,)),
         ],
         compiler_params=pltpu.CompilerParams(
-            collective_id=0, has_side_effects=True, vmem_limit_bytes=(20 if spaces <= 16 else 40) * 2**20),
+            collective_id=0, has_side_effects=True, vmem_limit_bytes=54 * 2**20),
         cost_estimate=pl.CostEstimate(
             flops=2 * count * width * 3 * width, bytes_accessed=6 * 2**20, transcendentals=0),
         name="pooled_keys",
@@ -365,7 +396,7 @@
     count, width = query.shape
     spots = pooled.shape[0]
     cols = tokens.shape[-1]
-    lines = math.gcd(count // cols, 2 if spots <= 512 else 1)
+    lines = math.gcd(count // cols, 4 if spots <= 512 else 1)
     block = pl.BlockSpec((lines * cols, width), lambda i: (i, 0))
     turned = pl.BlockSpec((lines, width, cols), lambda i: (i, 0, 0))
     vmem = pl.BlockSpec(memory_space=pltpu.VMEM)
@@ -382,7 +413,7 @@
             pltpu.VMEM((len(places), 2 * spots, size), BF16),
             pltpu.VMEM((len(places), 2 * spots, size), BF16),
         ],
-        compiler_params=pltpu.CompilerParams(vmem_limit_bytes=(24 if spots <= 512 else 52) * 2**20),
+        compiler_params=pltpu.CompilerParams(vmem_limit_bytes=(32 if spots <= 512 else 52) * 2**20),
         cost_estimate=pl.CostEstimate(
             flops=2 * count * width * (width + 2 * ffn + 2 * spots),
             bytes_accessed=10 * 2**20, transcendentals=count * (ffn + HEADS * spots)),

time: 43.2 us -> 42.2 us (0.977)
  local copies, waits for them, and re-layouts: 4.95 us -> 2.39 us
  Pallas kernels: 37.9 us -> 39.5 us
    pallas_call x1, Pallas kernels: 19.4 us -> 22.9 us  [pooled_keys(): pl.pallas_call(functools.partial(pooled_keys_kernel, rows_n, cols_n, HEAD...]
    unnamed x18 -> x12, local copies, waits for them, and re-layouts: 4.95 us -> 2.39 us
    pallas_call x1, Pallas kernels: 18.5 us -> 16.6 us  [finish(): pl.pallas_call(functools.partial(finish_kernel, HEADS), grid=(count // co...]
where the time goes in v3:
time: 42.2 us; the launch traced here: 42 us
  Pallas kernels  39.5 us (94%)
  local copies, waits for them, and re-layouts  2.39 us (6%)
    pallas_call x1, Pallas kernels, pooled_keys(): pl.pallas_call(functools.partial(pooled_keys_kernel, rows_n, cols_n, HEAD...  22.9 us
    pallas_call x1, Pallas kernels, finish(): pl.pallas_call(functools.partial(finish_kernel, HEADS), grid=(count // co...  16.6 us
    unnamed x12, local copies, waits for them, and re-layouts  2.39 us

profile of v3, /device:TPU:0, one launch (start us, length us, event | category | flops | bytes accessed | tf_op | source)
XLA Modules:
  0.0 42.0 jit_solution(2749928169178833010)
XLA Ops:
  0.0 0.0 copy-start
  0.0 0.0 copy-start.1
  0.0 0.0 copy-start.2
  0.0 0.0 copy-start.3
  0.0 22.9 %pooled_keys.1 = (bf16[1024,576]{1,0:T(8,128)(2,1)}, bf16[16,16,1152]{2,1,0:T(8,128)(2,1)}) custom-call(bf16[8,576,128]{2,1,0:T(8,128)(2,1)} %bitcast.8, bf16[576,1728]{1,0:T(8,128)(2,1)} %w_hbm.1, bf16[9,9,2,72]{3,2,1,0:T(2,128)(2,1)} %bitcast.11, f32[1,72]{1,0:T(1,128)} %bitcast.12, f32[1,72]{1,0:T(1,128)} %bitcast.13), custom_call_target="tpu_custom_call" | custom-call | flops 2038431744 | bytes 6291456 | tf_op jit(solution)/shard_map/pooled_keys/pallas_call | solution.py:269
  22.9 0.0 copy-done
  22.9 0.0 copy-done.1
  22.9 0.0 copy-done.2
  22.9 0.0 copy-done.3
  22.9 0.0 copy-start.4
  22.9 1.1 %copy-done.4 = bf16[16,16,1152]{2,1,0:T(8,128)(2,1)S(1)} copy-done((bf16[16,16,1152]{2,1,0:T(8,128)(2,1)S(1)}, bf16[16,16,1152]{2,1,0:T(8,128)(2,1)}, u32[]{:S(2)}) %copy-start.4) | copy-done | bytes 589848
  24.0 0.0 copy-start.5
  24.0 1.3 %copy-done.5 = bf16[1024,576]{1,0:T(8,128)(2,1)S(1)} copy-done((bf16[1024,576]{1,0:T(8,128)(2,1)S(1)}, bf16[1024,576]{1,0:T(8,128)(2,1)}, u32[]{:S(2)}) %copy-start.5) | copy-done | bytes 1179672
  25.3 16.6 %finish.1 = bf16[8,576,128]{2,1,0:T(8,128)(2,1)} custom-call(bf16[1024,576]{1,0:T(8,128)(2,1)S(1)} %copy-done.5, bf16[8,576,128]{2,1,0:T(8,128)(2,1)S(1)} %bitcast.9, bf16[256,1152]{1,0:T(8,128)(2,1)S(1)} %bitcast.10, bf16[576,576]{1,0:T(8,128)(2,1)S(1)} %copy-done.3, bf16[576,2304]{1,0:T(8,128)(2,1)S(1)} %copy-done, bf16[576,2304]{1,0:T(8,128)(2,1)S(1)} %bitcast.7), custom_call_target="tpu_custom_call" | custom-call | flops 6719275008 | bytes 10485760 | tf_op jit(solution)/shard_map/finish/pallas_call | solution.py:406
Async XLA Ops:
  0.0 22.9 %copy-start = (bf16[576,2304]{1,0:T(8,128)(2,1)S(1)}, bf16[576,2304]{1,0:T(8,128)(2,1)}, u32[]{:S(2)}) copy-start(bf16[576,2304]{1,0:T(8,128)(2,1)} %w_up_ref.1) | copy-start | bytes 7962628
  0.0 22.9 %copy-start.1 = (bf16[2304,576]{0,1:T(8,128)(2,1)S(1)}, bf16[2304,576]{0,1:T(8,128)(2,1)}, u32[]{:S(2)}) copy-start(bf16[2304,576]{0,1:T(8,128)(2,1)} %param.15) | copy-start | bytes 7962628
  0.0 22.9 %copy-start.2 = (bf16[8,128,576]{1,2,0:T(8,128)(2,1)S(1)}, bf16[8,128,576]{1,2,0:T(8,128)(2,1)}, u32[]{:S(2)}) copy-start(bf16[8,128,576]{1,2,0:T(8,128)(2,1)} %param.8) | copy-start | bytes 3538948
  0.0 22.9 %copy-start.3 = (bf16[576,576]{1,0:T(8,128)(2,1)S(1)}, bf16[576,576]{1,0:T(8,128)(2,1)}, u32[]{:S(2)}) copy-start(bf16[576,576]{1,0:T(8,128)(2,1)} %w_proj_ref.1) | copy-start | bytes 1990660
  22.9 1.1 %copy-start.4 = (bf16[16,16,1152]{2,1,0:T(8,128)(2,1)S(1)}, bf16[16,16,1152]{2,1,0:T(8,128)(2,1)}, u32[]{:S(2)}) copy-start(bf16[16,16,1152]{2,1,0:T(8,128)(2,1)} %get-tuple-element.8) | copy-start | bytes 1769476
  24.0 1.3 %copy-start.5 = (bf16[1024,576]{1,0:T(8,128)(2,1)S(1)}, bf16[1024,576]{1,0:T(8,128)(2,1)}, u32[]{:S(2)}) copy-start(bf16[1024,576]{1,0:T(8,128)(2,1)} %get-tuple-element.7.q_ref) | copy-start | bytes 3538948
